TPU v7x, 512 devices: a whole 4x4x16 slice. The times are simulated.
512 devices in a mesh: space: 64 (over y, z), dp: 8 (over x, core).
Axes of the slice: x: 4, y: 4, z: 16, core: 2. Of those that a mesh axis runs over, the one named last changes fastest.
Arguments:
- coarse_latents: bfloat16 [8, 4096, 512], P('dp', 'space'), may hold values from -6 to 6
- active_blocks: int32 [8, 128], P('dp'), may hold values from 0 to 4095, as said below
- face_links: int32 [8, 128, 6], P('dp', 'space'), may hold values from -1 to 127, as said below
- cotangent: bfloat16 [8, 128, 8, 8, 256], P('dp', 'space'), may hold values from -6 to 6
- up_weight: bfloat16 [64, 2048], replicated, may hold values from -0.75 to 0.75
- conv_one: bfloat16 [27, 32, 32], replicated, may hold values from -0.21875 to 0.21875
- conv_two: bfloat16 [27, 32, 32], replicated, may hold values from -0.21875 to 0.21875
Outputs:
- fine: bfloat16 [8, 128, 8, 8, 256], P('dp', 'space')
- grad_one: float32 [27, 32, 32], replicated
- grad_two: float32 [27, 32, 32], replicated
Inputs may be any that keep to these rules, and one draw needn't show every extreme that they name: `active_blocks`: call the bricks at positions i * 2 to (i + 1) * 2 - 1 group i and the block rows i * 64 to (i + 1) * 64 - 1 range i. At most 2 bricks of one group take their blocks from one range, and in every scene every group has exactly 2 from some range. `face_links`: links are mutual: if brick h is the neighbour of g across face f, g is the neighbour of h across the opposite face. A neighbour of brick g lies at a position whose quotient by 2 differs from that of g by at most one; across a -x, -y or -z face that quotient is never larger than that of g, across a +x, +y or +z face never smaller.
All inputs are finite; a program needn't handle non-finite values.
Results may differ from a plain program's by a relative error of at most 0.0057.
Values may be sent and summed in bfloat16 or wider, within the bound.
A program may use at most 128 MiB of HBM per device.

v0:
```python
import math
import jax
import jax.numpy as jnp
from jax import lax
from jax.sharding import PartitionSpec as P


def passed_along(value, axis, steps):
    count = lax.axis_size(axis)
    first, last = (max(0, -steps), min(count, count - steps))
    return lax.ppermute(value, axis, [(source, source + steps) for source in range(first, last)])


def depth_select(extent):
    inputs_z = jnp.arange(extent + 2)[None, :, None]
    outputs_z = jnp.arange(extent)[None, None, :]
    offsets_z = jnp.arange(3)[:, None, None]
    return (inputs_z == outputs_z + offsets_z).astype(jnp.float32)


def band_matrix(weights, extent):
    channels = weights.shape[1]
    cube = weights.astype(jnp.float32).reshape(3, 3, 3, channels, channels)
    banded = jnp.einsum(
        "dpq,abdio->abpiqo", depth_select(extent), cube, precision=lax.Precision.HIGHEST
    )
    return banded.reshape(3, 3, (extent + 2) * channels, extent * channels).astype(jnp.bfloat16)


def apply_band(padded, banded, extent):
    total = None
    for shift_x in range(3):
        for shift_y in range(3):
            window = padded[:, shift_x : shift_x + extent, shift_y : shift_y + extent, :]
            term = jnp.einsum(
                "nxyp,pq->nxyq",
                window,
                banded[shift_x, shift_y],
                preferred_element_type=jnp.float32,
            )
            total = term if total is None else total + term
    return total


def band_gradient(padded, gradient, extent, channels):
    select = depth_select(extent)
    pieces = []
    for shift_x in range(3):
        for shift_y in range(3):
            window = padded[:, shift_x : shift_x + extent, shift_y : shift_y + extent, :]
            outer = jnp.einsum(
                "nxyp,nxyq->pq", window, gradient, preferred_element_type=jnp.float32
            )
            outer = outer.reshape(extent + 2, channels, extent, channels)
            pieces.append(
                jnp.einsum("dpq,piqo->dio", select, outer, precision=lax.Precision.HIGHEST)
            )
    return jnp.stack(pieces).reshape(27, channels, channels)


def lift_bricks(latent_rows, up_weight, extent, channels):
    bricks_here = latent_rows.shape[0]
    blocks = latent_rows.reshape(bricks_here, 8, -1)
    cells = jnp.einsum("nci,io->nco", blocks, up_weight, preferred_element_type=jnp.float32)
    half = extent // 2
    shaped = cells.reshape(bricks_here, 2, 2, 2, half, half, half, channels)
    shaped = shaped.transpose(0, 1, 4, 2, 5, 3, 6, 7)
    return shaped.reshape(bricks_here, extent, extent, extent * channels).astype(jnp.bfloat16)


def face_planes(volume, channels):
    bricks_here, extent = (volume.shape[0], volume.shape[1])
    planes = [
        volume[:, 0],
        volume[:, extent - 1],
        volume[:, :, 0],
        volume[:, :, extent - 1],
        volume[:, :, :, 0:channels],
        volume[:, :, :, (extent - 1) * channels :],
    ]
    return jnp.stack([one_plane.reshape(bricks_here, -1) for one_plane in planes], axis=1)


def share_faces(stacked):
    from_left = passed_along(stacked, "space", 1)
    from_right = passed_along(stacked, "space", -1)
    return jnp.stack([from_left, stacked, from_right], axis=1)


def fill_padding(volume, face_pool, face_links, position, channels):
    bricks_here, extent = (volume.shape[0], volume.shape[1])
    neighbour = jnp.maximum(face_links, 0)
    source = jnp.clip(neighbour // bricks_here - position + 1, 0, 2)
    face_index = jnp.arange(6, dtype=jnp.int32)[None, :]
    row_index = (source * bricks_here + neighbour % bricks_here) * 6 + (face_index ^ 1)
    flattened = face_pool.reshape(3 * bricks_here * 6, -1)
    picked = jnp.take(flattened, row_index.reshape(-1), axis=0).reshape(bricks_here, 6, -1)
    picked = jnp.where((face_links >= 0)[:, :, None], picked, jnp.zeros((), picked.dtype))
    padded = jnp.pad(volume, ((0, 0), (1, 1), (1, 1), (channels, channels)))
    inside_range = slice(1, extent + 1)
    middle_range = slice(channels, (extent + 1) * channels)
    flat_face = (bricks_here, extent, extent * channels)
    depth_face = (bricks_here, extent, extent, channels)
    padded = padded.at[:, 0, inside_range, middle_range].set(picked[:, 0].reshape(flat_face))
    padded = padded.at[:, extent + 1, inside_range, middle_range].set(
        picked[:, 1].reshape(flat_face)
    )
    padded = padded.at[:, inside_range, 0, middle_range].set(picked[:, 2].reshape(flat_face))
    padded = padded.at[:, inside_range, extent + 1, middle_range].set(
        picked[:, 3].reshape(flat_face)
    )
    padded = padded.at[:, inside_range, inside_range, 0:channels].set(
        picked[:, 4].reshape(depth_face)
    )
    padded = padded.at[:, inside_range, inside_range, (extent + 1) * channels :].set(
        picked[:, 5].reshape(depth_face)
    )
    return padded


def body(coarse_latents, active_blocks, face_links, cotangent, up_weight, conv_one, conv_two):
    position = lax.axis_index("space")
    devices = lax.axis_size("space")
    bricks_here = face_links.shape[1]
    extent = cotangent.shape[2]
    channels = conv_one.shape[1]
    blocks_here = coarse_latents.shape[1]
    local_rows = coarse_latents[0]
    listed = active_blocks[0]
    mine = lax.dynamic_slice_in_dim(listed, position * bricks_here, bricks_here)
    owners = mine // blocks_here
    wanted = listed.reshape(devices, bricks_here)
    held = wanted // blocks_here == position
    local_index = jnp.clip(wanted - position * blocks_here, 0, blocks_here - 1)
    packed = jnp.where(
        held[:, :, None], jnp.take(local_rows, local_index, axis=0), jnp.zeros((), local_rows.dtype)
    )
    received = lax.all_to_all(packed, "space", split_axis=0, concat_axis=0, tiled=True)
    latent_rows = received[owners, jnp.arange(bricks_here)]
    lifted = lift_bricks(latent_rows, up_weight, extent, channels)
    links = face_links[0]
    upstream = cotangent[0]
    lifted_pool = share_faces(face_planes(lifted, channels)[None])[0]
    lifted_pad = fill_padding(lifted, lifted_pool, links, position, channels)
    band_one = band_matrix(conv_one, extent)
    band_two = band_matrix(conv_two, extent)
    band_back = band_matrix(jnp.flip(conv_two, axis=0).transpose(0, 2, 1), extent)
    pre = apply_band(lifted_pad, band_one, extent)
    hidden = jax.nn.silu(pre).astype(jnp.bfloat16)
    hidden_pool = share_faces(face_planes(hidden, channels)[None])[0]
    hidden_pad = fill_padding(hidden, hidden_pool, links, position, channels)
    fine = (lifted.astype(jnp.float32) + apply_band(hidden_pad, band_two, extent)).astype(
        jnp.bfloat16
    )
    scale = 1.0 / math.sqrt(lax.axis_size("dp") * devices * bricks_here * extent**3)
    second_local = band_gradient(hidden_pad, upstream, extent, channels) * scale
    upstream_pool = share_faces(face_planes(upstream, channels)[None])[0]
    upstream_pad = fill_padding(upstream, upstream_pool, links, position, channels)
    back = apply_band(upstream_pad, band_back, extent)
    sigmoid = jax.nn.sigmoid(pre)
    grad_pre = (back * sigmoid * (1.0 + pre * (1.0 - sigmoid))).astype(jnp.bfloat16)
    first_local = band_gradient(lifted_pad, grad_pre, extent, channels) * scale
    grad_one, grad_two = lax.psum((first_local, second_local), ("space", "dp"))
    return (fine[None], grad_one, grad_two)


def solution(mesh):
    return jax.shard_map(
        body,
        mesh=mesh,
        in_specs=(
            P("dp", "space", None),
            P("dp", None),
            P("dp", "space", None),
            P("dp", "space", None, None, None),
            P(),
            P(),
            P(),
        ),
        out_specs=(P("dp", "space", None, None, None), P(), P()),
        check_vma=False,
    )
```

profile of v0, /device:TPU:1, one launch (start us, length us, event | category | flops | bytes accessed | tf_op | source)
XLA Modules:
  0.0 758.2 jit_solution(1332796535409045901)
XLA Ops:
  13.7 5.0 collective-permute-start.4
  25.9 19.5 %all-to-all-start = ((bf16[64,2,512]{2,1,0:T(2,128)(2,1)}), bf16[64,2,512]{2,1,0:T(2,128)(2,1)S(1)}, u32[]{:S(2)}, u32[]{:S(2)}) async-start(bf16[64,2,512]{2,1,0:T(2,128)(2,1)} %broadcast_select_fusion.1), calls=%async_computation | async-start | bytes 262144 | tf_op jit(solution)/shard_map/all_to_all | solution.py:138
  45.5 5.6 convert_bitcast_fusion.2
  51.7 5.7 convert_bitcast_fusion
  57.4 2.0 all-to-all-done
  65.3 3.2 collective-permute-start
  70.2 5.6 convert_bitcast_fusion.1
  75.8 10.3 %copy.127 = bf16[3,3,10,32,8,32]{5,4,3,2,1,0:T(8,128)(2,1)} copy(bf16[3,3,10,32,8,32]{5,2,3,1,0,4:T(8,128)(2,1)} %convert_bitcast_fusion.2) | data formatting | bytes 2949120 | tf_op jit(solution)/shard_map/convert_element_type | solution.py:27
  86.2 7.2 convert_element_type.66
  93.7 10.3 %copy.141 = bf16[3,3,10,32,8,32]{5,4,3,2,1,0:T(8,128)(2,1)} copy(bf16[3,3,10,32,8,32]{5,2,3,1,0,4:T(8,128)(2,1)} %convert_bitcast_fusion) | data formatting | bytes 2949120 | tf_op jit(solution)/shard_map/convert_element_type | solution.py:27
  103.9 8.3 %convert_element_type.74 = bf16[3,3,320,256]{3,2,1,0:T(8,128)(2,1)} reshape(bf16[3,3,10,32,8,32]{5,4,3,2,1,0:T(8,128)(2,1)} %copy.141) | data formatting | bytes 2949120 | tf_op jit(solution)/shard_map/convert_element_type | solution.py:27
  112.2 10.4 %copy.134 = bf16[3,3,10,32,8,32]{5,4,3,2,1,0:T(8,128)(2,1)} copy(bf16[3,3,10,32,8,32]{5,2,3,1,0,4:T(8,128)(2,1)} %convert_bitcast_fusion.1) | data formatting | bytes 2949120 | tf_op jit(solution)/shard_map/convert_element_type | solution.py:27
  122.6 7.2 convert_element_type.70
  134.0 2.2 gather_fusion.2
  142.1 3.0 scatter.60
  145.1 2.9 scatter.61
  148.0 4.0 scatter.64
  152.0 4.0 scatter.65
  156.0 2.9 scatter.66
  158.9 5.7 scatter.69
  170.3 4.0 collective-permute-start.2
  182.9 2.7 scatter.84
  185.6 2.7 scatter.85
  189.0 5.0 scatter.89
  215.4 2.7 scatter.74
  218.1 2.7 scatter.75
  221.5 5.4 scatter.79
  231.5 2.2 fusion.72
  235.2 2.2 fusion.75
  239.0 2.2 fusion.78
  274.7 2.2 fusion.45
  283.1 464.4 %all-reduce.6.cloned.1.call-done = (f32[27,32,32]{2,1,0:T(8,128)}, f32[27,32,32]{2,1,0:T(8,128)}) async-done(((f32[27,32,32]{2,1,0:T(8,128)}, f32[27,32,32]{2,1,0:T(8,128)}), (f32[27,32,32]{2,1,0:T(8,128)}, f32[27,32,32]{2,1,0:T(8,128)})) %all-reduce.6.cloned.1.call-update) | async-done | bytes 221200 | tf_op jit(solution)/shard_map/psum | solution.py:163
  (269 shorter events, 119.6 us)
Async XLA Ops:
  7.2 16.7 %copy-start = (bf16[1,64,512]{2,1,0:T(8,128)(2,1)S(1)}, bf16[1,64,512]{2,1,0:T(8,128)(2,1)}, u32[]{:S(2)}) copy-start(bf16[1,64,512]{2,1,0:T(8,128)(2,1)} %param.45) | copy-start | bytes 196612
  7.2 38.3 %copy-start.8 = (bf16[27,32,32]{2,1,0:T(8,128)(2,1)S(1)}, bf16[27,32,32]{2,1,0:T(8,128)(2,1)}, u32[]{:S(2)}) copy-start(bf16[27,32,32]{2,1,0:T(8,128)(2,1)} %param.50) | copy-start | bytes 165892
  13.7 162.2 %collective-permute-start.4 = (bf16[1,2,6,2048]{3,1,2,0:T(2,128)(2,1)}, bf16[1,2,6,2048]{3,1,2,0:T(2,128)(2,1)}, u32[]{:S(2)}, u32[]{:S(2)}) collective-permute-start(bf16[1,2,6,2048]{3,1,2,0:T(2,128)(2,1)} %bitcast.92), channel_id=1, source_target_pairs={{0,8},{8,16},{16,24},{24,32},{32,40},{40,48},{48,56},{56,64},{64,7... | collective-permute-start | bytes 147464 | tf_op jit(solution)/shard_map/ppermute | solution.py:11
  18.7 157.2 %collective-permute-start.5 = (bf16[1,2,6,2048]{3,1,2,0:T(2,128)(2,1)}, bf16[1,2,6,2048]{3,1,2,0:T(2,128)(2,1)}, u32[]{:S(2)}, u32[]{:S(2)}) collective-permute-start(bf16[1,2,6,2048]{3,1,2,0:T(2,128)(2,1)} %bitcast.92), channel_id=1, source_target_pairs={{8,0},{16,8},{24,16},{32,24},{40,32},{48,40},{56,48},{64,56},{72,6... | collective-permute-start | bytes 147464 | tf_op jit(solution)/shard_map/ppermute | solution.py:11
  21.3 116.5 %copy-start.16 = (pred[2,6]{1,0:T(4,128)(4,1)}, pred[2,6]{1,0:T(4,128)(4,1)S(1)}, u32[]{:S(2)}) copy-start(pred[2,6]{1,0:T(4,128)(4,1)S(1)} %get-tuple-element.285) | copy-start | bytes 40
  23.8 112.4 %copy-start.14 = (pred[12]{0:T(512)(128)(4,1)}, pred[12]{0:T(512)(128)(4,1)S(1)}, u32[]{:S(2)}) copy-start(pred[12]{0:T(512)(128)(4,1)S(1)} %get-tuple-element.242) | copy-start | bytes 40
  25.9 33.5 %all-to-all-start = ((bf16[64,2,512]{2,1,0:T(2,128)(2,1)}), bf16[64,2,512]{2,1,0:T(2,128)(2,1)S(1)}, u32[]{:S(2)}, u32[]{:S(2)}) async-start(bf16[64,2,512]{2,1,0:T(2,128)(2,1)} %broadcast_select_fusion.1), calls=%async_computation | async-start | bytes 262144 | tf_op jit(solution)/shard_map/all_to_all | solution.py:138
  45.4 702.1 %all-reduce.6.cloned.1.call-start = ((), (), s32[]{:S(2)}) async-start(), calls=%async_computation.1 | async-start | bytes 1769472 | tf_op jit(solution)/shard_map/psum | solution.py:163
  45.5 5.6 copy-start.18
  45.5 5.7 copy-start.9
  45.5 6.0 copy-start.6
  61.2 68.5 %copy-start.4 = (bf16[2,8,8,256]{3,2,1,0:T(8,128)(2,1)}, bf16[2,8,8,256]{3,2,1,0:T(8,128)(2,1)S(1)}, u32[]{:S(2)}) copy-start(bf16[2,8,8,256]{3,2,1,0:T(8,128)(2,1)S(1)} %convert_element_type.62) | copy-start | bytes 196612
  65.3 65.3 %collective-permute-start = (bf16[1,2,6,2048]{3,1,2,0:T(2,128)(2,1)}, bf16[1,2,6,2048]{3,1,2,0:T(2,128)(2,1)}, u32[]{:S(2)}, u32[]{:S(2)}) collective-permute-start(bf16[1,2,6,2048]{3,1,2,0:T(2,128)(2,1)} %bitcast.10), channel_id=1, source_target_pairs={{0,8},{8,16},{16,24},{24,32},{32,40},{40,48},{48,56},{56,64},{64,7... | collective-permute-start | bytes 147464 | tf_op jit(solution)/shard_map/ppermute | solution.py:11
  68.5 62.1 %collective-permute-start.1 = (bf16[1,2,6,2048]{3,1,2,0:T(2,128)(2,1)}, bf16[1,2,6,2048]{3,1,2,0:T(2,128)(2,1)}, u32[]{:S(2)}, u32[]{:S(2)}) collective-permute-start(bf16[1,2,6,2048]{3,1,2,0:T(2,128)(2,1)} %bitcast.10), channel_id=1, source_target_pairs={{8,0},{16,8},{24,16},{32,24},{40,32},{48,40},{56,48},{64,56},{72,6... | collective-permute-start | bytes 147464 | tf_op jit(solution)/shard_map/ppermute | solution.py:11
  86.2 7.2 copy-start.7
  164.6 3.4 copy-start.2
  170.3 7.5 collective-permute-start.2
  174.3 4.8 collective-permute-start.3
  177.0 3.1 copy-start.15
  177.1 3.2 copy-start.17
  196.2 6.7 copy-start.19
  199.6 4.5 copy-start.3
  250.8 1.6 copy-start.10
  250.9 1.6 copy-start.11
  250.9 1.6 copy-start.12
  278.2 1.6 copy-start.13
  281.5 0.8 copy-start.5
  282.2 468.9 %copy-start.1 = (bf16[1,64,512]{2,1,0:T(8,128)(2,1)S(1)}, bf16[1,64,512]{2,1,0:T(8,128)(2,1)}, u32[]{:S(2)}) copy-start(bf16[1,64,512]{2,1,0:T(8,128)(2,1)} %param.45) | copy-start | bytes 196612
Sparse Core Ops, SparseCore 0:
  282.4 465.0 all-reduce.5
where the time goes:
time: 766 us; the launch traced here: 758 us
  waiting for transfers between devices  468 us (61%)
  local copies, waits for them, and re-layouts  151 us (20%)
  matrix products  77.9 us (10%)
  starting transfers between devices  36.3 us (5%)
  between operations  15.5 us (2%)
  other arithmetic  9.85 us (1%)
    psum x1, waiting for transfers between devices, body(): grad_one, grad_two = lax.psum((first_local, second_local), ('space', 'dp'))  464 us
    convert_element_type x6, local copies, waits for them, and re-layouts, band_matrix(): banded.reshape(3, 3, (extent + 2) * channels, extent * channels)  53.6 us
    dot_general x18, matrix products, band_gradient(): jnp.einsum('dpq,piqo->dio', select, outer, precision=lax.Precision.HIGHEST)  30.7 us
    all_to_all x1, starting transfers between devices, body(): lax.all_to_all(packed, 'space', split_axis=0, concat_axis=0, tiled=True)  19.5 us
    dot_general x27, matrix products, apply_band(): jnp.einsum('nxyp,pq->nxyq', window, banded[shift_x, shift_y], preferred_e...  17.4 us
    dot_general x3, matrix products, band_matrix(): jnp.einsum('dpq,abdio->abpiqo', depth_select(extent), cube, precision=lax...  16.8 us
    ppermute x6, starting transfers between devices, passed_along(): lax.ppermute(value, axis, [(source, source + steps) for source in range(f...  16.7 us
    scatter x3, local copies, waits for them, and re-layouts, fill_padding(): padded.at[:, inside_range, inside_range, (extent + 1) * channels:]  16.1 us
  transfers between devices with their start and end apart: 8, of which 3 were waited for; matrix products, arithmetic and copies ran while one was open for 17% of the time, Pallas kernels for 0%

commit v1 on v0

--- a/solution.py
+++ b/solution.py
@@ -160,7 +160,7 @@
     sigmoid = jax.nn.sigmoid(pre)
     grad_pre = (back * sigmoid * (1.0 + pre * (1.0 - sigmoid))).astype(jnp.bfloat16)
     first_local = band_gradient(lifted_pad, grad_pre, extent, channels) * scale
-    grad_one, grad_two = lax.psum((first_local, second_local), ("space", "dp"))
+    grad_one, grad_two = lax.psum(lax.psum((first_local, second_local), "dp"), "space")
     return (fine[None], grad_one, grad_two)
 
 

time: 766 us -> 654 us (0.85)
  the two profiles are of different devices: /device:TPU:1 before, /device:TPU:2 now
where the time goes in v1:
time: 654 us; the launch traced here: 646 us
  waiting for transfers between devices  355 us (54%)
  local copies, waits for them, and re-layouts  151 us (23%)
  matrix products  77.9 us (12%)
  starting transfers between devices  37.1 us (6%)
  between operations  15.6 us (2%)
  other arithmetic  9.85 us (2%)
    psum x1, waiting for transfers between devices, body(): lax.psum(lax.psum((first_local, second_local), 'dp'), 'space')  275 us
    psum x1, waiting for transfers between devices, body(): lax.psum((first_local, second_local), 'dp')  73.5 us
    convert_element_type x6, local copies, waits for them, and re-layouts, band_matrix(): banded.reshape(3, 3, (extent + 2) * channels, extent * channels)  53.6 us
    dot_general x18, matrix products, band_gradient(): jnp.einsum('dpq,piqo->dio', select, outer, precision=lax.Precision.HIGHEST)  30.7 us
    all_to_all x1, starting transfers between devices, body(): lax.all_to_all(packed, 'space', split_axis=0, concat_axis=0, tiled=True)  20.1 us
    dot_general x27, matrix products, apply_band(): jnp.einsum('nxyp,pq->nxyq', window, banded[shift_x, shift_y], preferred_e...  17.4 us
    ppermute x6, starting transfers between devices, passed_along(): lax.ppermute(value, axis, [(source, source + steps) for source in range(f...  16.9 us
    dot_general x3, matrix products, band_matrix(): jnp.einsum('dpq,abdio->abpiqo', depth_select(extent), cube, precision=lax...  16.8 us
  transfers between devices with their start and end apart: 9, of which 4 were waited for; matrix products, arithmetic and copies ran while one was open for 20% of the time, Pallas kernels for 0%

profile of v1, /device:TPU:2, one launch (start us, length us, event | category | flops | bytes accessed | tf_op | source)
XLA Modules:
  0.0 646.3 jit_solution(12702054438642683129)
XLA Ops:
  13.7 4.4 collective-permute-start.4
  25.4 20.1 %all-to-all-start = ((bf16[64,2,512]{2,1,0:T(2,128)(2,1)}), bf16[64,2,512]{2,1,0:T(2,128)(2,1)S(1)}, u32[]{:S(2)}, u32[]{:S(2)}) async-start(bf16[64,2,512]{2,1,0:T(2,128)(2,1)} %broadcast_select_fusion.1), calls=%async_computation | async-start | bytes 262144 | tf_op jit(solution)/shard_map/all_to_all | solution.py:138
  45.5 5.6 convert_bitcast_fusion.2
  51.7 5.7 convert_bitcast_fusion
  57.4 4.0 all-to-all-done
  67.2 3.4 collective-permute-start
  72.4 5.6 convert_bitcast_fusion.1
  78.0 10.3 %copy.127 = bf16[3,3,10,32,8,32]{5,4,3,2,1,0:T(8,128)(2,1)} copy(bf16[3,3,10,32,8,32]{5,2,3,1,0,4:T(8,128)(2,1)} %convert_bitcast_fusion.2) | data formatting | bytes 2949120 | tf_op jit(solution)/shard_map/convert_element_type | solution.py:27
  88.4 7.2 %convert_element_type.66 = bf16[3,3,320,256]{3,2,1,0:T(8,128)(2,1)S(1)} reshape(bf16[3,3,10,32,8,32]{5,4,3,2,1,0:T(8,128)(2,1)} %copy.127) | data formatting | bytes 2949120 | tf_op jit(solution)/shard_map/convert_element_type | solution.py:27
  95.9 10.3 %copy.141 = bf16[3,3,10,32,8,32]{5,4,3,2,1,0:T(8,128)(2,1)} copy(bf16[3,3,10,32,8,32]{5,2,3,1,0,4:T(8,128)(2,1)} %convert_bitcast_fusion) | data formatting | bytes 2949120 | tf_op jit(solution)/shard_map/convert_element_type | solution.py:27
  106.1 8.3 %convert_element_type.74 = bf16[3,3,320,256]{3,2,1,0:T(8,128)(2,1)} reshape(bf16[3,3,10,32,8,32]{5,4,3,2,1,0:T(8,128)(2,1)} %copy.141) | data formatting | bytes 2949120 | tf_op jit(solution)/shard_map/convert_element_type | solution.py:27
  114.4 10.4 %copy.134 = bf16[3,3,10,32,8,32]{5,4,3,2,1,0:T(8,128)(2,1)} copy(bf16[3,3,10,32,8,32]{5,2,3,1,0,4:T(8,128)(2,1)} %convert_bitcast_fusion.1) | data formatting | bytes 2949120 | tf_op jit(solution)/shard_map/convert_element_type | solution.py:27
  124.7 7.2 %convert_element_type.70 = bf16[3,3,320,256]{3,2,1,0:T(8,128)(2,1)S(1)} reshape(bf16[3,3,10,32,8,32]{5,4,3,2,1,0:T(8,128)(2,1)} %copy.134) | data formatting | bytes 2949120 | tf_op jit(solution)/shard_map/convert_element_type | solution.py:27
  136.2 2.2 gather_fusion.2
  144.3 3.0 scatter.60
  147.2 2.9 scatter.61
  150.2 4.0 scatter.64
  154.2 4.0 scatter.65
  158.1 2.9 scatter.66
  161.1 5.7 scatter.69
  172.5 4.5 collective-permute-start.2
  180.6 2.5 collective-permute-done.3
  186.7 2.7 scatter.84
  189.5 2.7 scatter.85
  192.9 5.0 scatter.89
  219.3 2.7 scatter.74
  222.0 2.7 scatter.75
  225.4 5.4 scatter.79
  235.4 2.2 fusion.72
  278.6 2.2 fusion.45
  286.0 73.5 %all-reduce.10.cloned.1.call-done = (f32[27,32,32]{2,1,0:T(8,128)}, f32[27,32,32]{2,1,0:T(8,128)}) async-done(((f32[27,32,32]{2,1,0:T(8,128)}, f32[27,32,32]{2,1,0:T(8,128)}), (f32[27,32,32]{2,1,0:T(8,128)}, f32[27,32,32]{2,1,0:T(8,128)})) %all-reduce.10.cloned.1.call-update) | async-done | bytes 221200 | tf_op jit(solution)/shard_map/psum | solution.py:163
  360.5 275.1 %all-reduce.8.cloned.1.call-done = (f32[27,32,32]{2,1,0:T(8,128)}, f32[27,32,32]{2,1,0:T(8,128)}) async-done(((f32[27,32,32]{2,1,0:T(8,128)}, f32[27,32,32]{2,1,0:T(8,128)}), (f32[27,32,32]{2,1,0:T(8,128)}, f32[27,32,32]{2,1,0:T(8,128)})) %all-reduce.8.cloned.1.call-update) | async-done | bytes 221200 | tf_op jit(solution)/shard_map/psum | solution.py:163
  (272 shorter events, 122.6 us)
Async XLA Ops:
  7.2 16.1 %copy-start = (bf16[1,64,512]{2,1,0:T(8,128)(2,1)S(1)}, bf16[1,64,512]{2,1,0:T(8,128)(2,1)}, u32[]{:S(2)}) copy-start(bf16[1,64,512]{2,1,0:T(8,128)(2,1)} %param.45) | copy-start | bytes 196612
  7.2 38.3 %copy-start.8 = (bf16[27,32,32]{2,1,0:T(8,128)(2,1)S(1)}, bf16[27,32,32]{2,1,0:T(8,128)(2,1)}, u32[]{:S(2)}) copy-start(bf16[27,32,32]{2,1,0:T(8,128)(2,1)} %param.50) | copy-start | bytes 165892
  13.7 164.9 %collective-permute-start.4 = (bf16[1,2,6,2048]{3,1,2,0:T(2,128)(2,1)}, bf16[1,2,6,2048]{3,1,2,0:T(2,128)(2,1)}, u32[]{:S(2)}, u32[]{:S(2)}) collective-permute-start(bf16[1,2,6,2048]{3,1,2,0:T(2,128)(2,1)} %bitcast.92), channel_id=1, source_target_pairs={{0,8},{8,16},{16,24},{24,32},{32,40},{40,48},{48,56},{56,64},{64,7... | collective-permute-start | bytes 147464 | tf_op jit(solution)/shard_map/ppermute | solution.py:11
  18.1 160.5 %collective-permute-start.5 = (bf16[1,2,6,2048]{3,1,2,0:T(2,128)(2,1)}, bf16[1,2,6,2048]{3,1,2,0:T(2,128)(2,1)}, u32[]{:S(2)}, u32[]{:S(2)}) collective-permute-start(bf16[1,2,6,2048]{3,1,2,0:T(2,128)(2,1)} %bitcast.92), channel_id=1, source_target_pairs={{8,0},{16,8},{24,16},{32,24},{40,32},{48,40},{56,48},{64,56},{72,6... | collective-permute-start | bytes 147464 | tf_op jit(solution)/shard_map/ppermute | solution.py:11
  20.8 119.2 %copy-start.16 = (pred[2,6]{1,0:T(4,128)(4,1)}, pred[2,6]{1,0:T(4,128)(4,1)S(1)}, u32[]{:S(2)}) copy-start(pred[2,6]{1,0:T(4,128)(4,1)S(1)} %get-tuple-element.287) | copy-start | bytes 40
  23.3 115.1 %copy-start.14 = (pred[12]{0:T(512)(128)(4,1)}, pred[12]{0:T(512)(128)(4,1)S(1)}, u32[]{:S(2)}) copy-start(pred[12]{0:T(512)(128)(4,1)S(1)} %get-tuple-element.244) | copy-start | bytes 40
  25.4 36.0 %all-to-all-start = ((bf16[64,2,512]{2,1,0:T(2,128)(2,1)}), bf16[64,2,512]{2,1,0:T(2,128)(2,1)S(1)}, u32[]{:S(2)}, u32[]{:S(2)}) async-start(bf16[64,2,512]{2,1,0:T(2,128)(2,1)} %broadcast_select_fusion.1), calls=%async_computation | async-start | bytes 262144 | tf_op jit(solution)/shard_map/all_to_all | solution.py:138
  45.4 314.0 %all-reduce.10.cloned.1.call-start = ((), (), s32[]{:S(2)}) async-start(), calls=%async_computation.2 | async-start | bytes 1769472 | tf_op jit(solution)/shard_map/psum | solution.py:163
  45.5 5.6 copy-start.18
  45.5 5.7 copy-start.9
  45.5 6.0 copy-start.6
  63.1 68.8 %copy-start.4 = (bf16[2,8,8,256]{3,2,1,0:T(8,128)(2,1)}, bf16[2,8,8,256]{3,2,1,0:T(8,128)(2,1)S(1)}, u32[]{:S(2)}) copy-start(bf16[2,8,8,256]{3,2,1,0:T(8,128)(2,1)S(1)} %convert_element_type.62) | copy-start | bytes 196612
  67.2 65.5 %collective-permute-start = (bf16[1,2,6,2048]{3,1,2,0:T(2,128)(2,1)}, bf16[1,2,6,2048]{3,1,2,0:T(2,128)(2,1)}, u32[]{:S(2)}, u32[]{:S(2)}) collective-permute-start(bf16[1,2,6,2048]{3,1,2,0:T(2,128)(2,1)} %bitcast.10), channel_id=1, source_target_pairs={{0,8},{8,16},{16,24},{24,32},{32,40},{40,48},{48,56},{56,64},{64,7... | collective-permute-start | bytes 147464 | tf_op jit(solution)/shard_map/ppermute | solution.py:11
  70.7 62.1 %collective-permute-start.1 = (bf16[1,2,6,2048]{3,1,2,0:T(2,128)(2,1)}, bf16[1,2,6,2048]{3,1,2,0:T(2,128)(2,1)}, u32[]{:S(2)}, u32[]{:S(2)}) collective-permute-start(bf16[1,2,6,2048]{3,1,2,0:T(2,128)(2,1)} %bitcast.10), channel_id=1, source_target_pairs={{8,0},{16,8},{24,16},{32,24},{40,32},{48,40},{56,48},{64,56},{72,6... | collective-permute-start | bytes 147464 | tf_op jit(solution)/shard_map/ppermute | solution.py:11
  88.4 7.2 %copy-start.7 = (bf16[1,2,8,8,256]{4,3,2,1,0:T(8,128)(2,1)S(1)}, bf16[1,2,8,8,256]{4,3,2,1,0:T(8,128)(2,1)}, u32[]{:S(2)}) copy-start(bf16[1,2,8,8,256]{4,3,2,1,0:T(8,128)(2,1)} %param.48) | copy-start | bytes 196612
  166.8 3.4 copy-start.2
  172.5 8.0 %collective-permute-start.2 = (bf16[1,2,6,2048]{3,1,2,0:T(2,128)(2,1)S(1)}, bf16[1,2,6,2048]{3,1,2,0:T(2,128)(2,1)S(1)}, u32[]{:S(2)}, u32[]{:S(2)}) collective-permute-start(bf16[1,2,6,2048]{3,1,2,0:T(2,128)(2,1)S(1)} %bitcast.663), channel_id=1, source_target_pairs={{0,8},{8,16},{16,24},{24,32},{32,40},{40,48},{48,56},{56,64},{64,7... | collective-permute-start | bytes 147464 | tf_op jit(solution)/shard_map/ppermute | solution.py:11
  177.1 6.0 collective-permute-start.3
  179.8 4.3 copy-start.15
  179.8 4.3 copy-start.17
  200.1 6.7 %copy-start.19 = (f32[2,8,8,256]{3,2,1,0:T(8,128)S(1)}, f32[2,8,8,256]{3,2,1,0:T(8,128)}, u32[]{:S(2)}) copy-start(f32[2,8,8,256]{3,2,1,0:T(8,128)} %get-tuple-element.296) | copy-start | bytes 393220
  203.5 4.5 copy-start.3
  254.7 1.6 copy-start.10
  254.7 1.6 copy-start.11
  254.8 1.6 copy-start.12
  282.1 1.6 copy-start.13
  285.7 74.0 %copy-start.5 = (bf16[2,8,8,256]{3,2,1,0:T(8,128)(2,1)S(1)}, bf16[2,8,8,256]{3,2,1,0:T(8,128)(2,1)}, u32[]{:S(2)}) copy-start(bf16[2,8,8,256]{3,2,1,0:T(8,128)(2,1)} %copy-done.4) | copy-start | bytes 196612
  285.8 349.8 %all-reduce.8.cloned.1.call-start = ((), (), s32[]{:S(2)}) async-start(), calls=%async_computation.1 | async-start | bytes 1769472 | tf_op jit(solution)/shard_map/psum | solution.py:163
  359.5 279.7 %copy-start.1 = (bf16[1,64,512]{2,1,0:T(8,128)(2,1)S(1)}, bf16[1,64,512]{2,1,0:T(8,128)(2,1)}, u32[]{:S(2)}) copy-start(bf16[1,64,512]{2,1,0:T(8,128)(2,1)} %param.45) | copy-start | bytes 196612
Sparse Core Ops, SparseCore 0:
  285.9 73.5 all-reduce.9
  363.2 272.2 all-reduce.7
